TPU v7x, 128 devices: a whole 4x4x4 slice. The times are simulated.
128 devices in a mesh: fsdp: 16 (over y_hi, z, core), tp: 8 (over x, y_lo).
Axes of the slice: x: 4, y: 4 (y_hi: 2, y_lo: 2; y = y_hi * 2 + y_lo), z: 4, core: 2. Of those that a mesh axis runs over, the one named last changes fastest.
Arguments:
- normed: bfloat16 [2, 256, 16384], P(None, None, 'fsdp'), may hold values from -6 to 6
- resident_gate_matrix: bfloat16 [16384, 26624], P('fsdp', 'tp'), may hold values from -0.046875 to 0.046875
- resident_up_matrix: bfloat16 [16384, 26624], P('fsdp', 'tp'), may hold values from -0.046875 to 0.046875
- resident_down_matrix: bfloat16 [26624, 16384], P('tp', 'fsdp'), may hold values from -0.0390625 to 0.0390625
- gate_input_factor: bfloat16 [16, 16384], P(None, ('fsdp', 'tp')), may hold values from -0.046875 to 0.046875
- up_input_factor: bfloat16 [16, 16384], P(None, ('fsdp', 'tp')), may hold values from -0.046875 to 0.046875
- gate_output_factor: bfloat16 [26624, 16], P(('tp', 'fsdp')), may hold values from -0.29882812 to 0.29882812
- up_output_factor: bfloat16 [26624, 16], P(('tp', 'fsdp')), may hold values from -0.29882812 to 0.29882812
- down_input_factor: bfloat16 [16, 26624], P(None, ('tp', 'fsdp')), may hold values from -0.0390625 to 0.0390625
- down_output_factor: bfloat16 [16384, 16], P(('fsdp', 'tp')), may hold values from -0.29882812 to 0.29882812
Outputs:
- mixed: bfloat16 [2, 256, 16384], P(None, 'tp', 'fsdp')
All inputs are finite; a program needn't handle non-finite values.
Results may differ from a plain program's by a relative error of at most 0.007.
Values may be sent and summed in bfloat16 or wider, within the bound.
No kernel may reach another device: no remote copies, remote signals or barrier semaphores. Data moves between devices by JAX's collectives and lax.ppermute only.
A program may use at most 128 MiB of HBM per device.

v0:
```python
import functools

import jax
import jax.numpy as jnp
from jax import lax
from jax.experimental import pallas as pl
from jax.experimental.pallas import tpu as pltpu
from jax.sharding import Mesh
from jax.sharding import PartitionSpec as P

adapter_scale = 2.0
f32 = jnp.float32
bf16 = jnp.bfloat16
FSDP = ("yh", "z", "c")
TP = ("x", "yl")
RANK = 16
VMEM_LIMIT = 16 * 1024 * 1024


def pair_bits(core):
    return 1 + 2 * core, 3 - 2 * core


def owner(r, y_first):
    yh, z, c = lax.axis_index("yh"), lax.axis_index("z"), lax.axis_index("c")
    core, bits = (r >> 3) & 1, ((r >> 2) & 1, (r >> 1) & 1, r & 1)
    y, first_z, second_z = bits if y_first else (bits[2], bits[0], bits[1])
    cc = c ^ core
    a, b = pair_bits(cc)
    zz = z ^ (first_z * a) ^ (second_z * b)
    return ((yh ^ y) * 4 + zz) * 2 + cc


def swap(axis, value):
    return lax.ppermute(value, axis, [(0, 1), (1, 0)])


def ring_pair(axis, first, value):
    axes = ("z", "c") if axis == "z" else ("c", "x")

    def index(place, core):
        return place * 2 + core if axis == "z" else core * 4 + place

    moves = []
    for place in range(4):
        for core in range(2):
            step = pair_bits(core)[0 if first else 1]
            moves.append((index(place, core), index(place ^ step, core)))
    return lax.ppermute(value, axes, moves)


def xor_pair(axis, step, value):
    return lax.ppermute(value, axis, [(i, i ^ step) for i in range(4)])


def exchange(axes, value):
    return lax.all_to_all(value, axes, split_axis=0, concat_axis=0)


def in_vmem(body, name, out_shape, *args, behind=(), token=False):
    whole = pl.BlockSpec(memory_space=pltpu.VMEM)
    if token:
        out_shape = (*out_shape, ((8, 128), f32))
    outs = tuple(jax.ShapeDtypeStruct(shape, dtype) for shape, dtype in out_shape)
    moved = sum(a.size * a.dtype.itemsize for a in (*args, *outs))

    def kernel(*refs):
        out_refs = refs[len(args) + len(behind) :]
        if token:
            out_refs[-1][...] = jnp.zeros((8, 128), f32)
            out_refs = out_refs[:-1]
        body(*refs[: len(args)], *out_refs)

    return pl.pallas_call(
        kernel,
        in_specs=[whole] * (len(args) + len(behind)),
        out_specs=[whole] * len(outs),
        out_shape=outs,
        compiler_params=pltpu.CompilerParams(vmem_limit_bytes=VMEM_LIMIT),
        cost_estimate=pl.CostEstimate(flops=moved, bytes_accessed=moved, transcendentals=0),
        name=name,
    )(*args, *behind)


def rows_at(block, size):
    return pl.ds(pl.multiple_of(block * size, 16), size)


def other_core_body(size, y_first, part_ref, send_ref):
    for r in range(8):
        send_ref[r * size : (r + 1) * size] = part_ref[rows_at(owner(8 + r, y_first), size), :]


def core_sum_body(size, y_first, part_ref, recv_ref, keep_ref, send_ref):
    for r in range(8):
        at = r * size
        mine = rows_at(owner(r, y_first), size)
        total = part_ref[mine, :].astype(f32) + recv_ref[at : at + size].astype(f32)
        if r < 4:
            keep_ref[at : at + size] = total
        else:
            send_ref[at - 4 * size : at - 3 * size] = total.astype(bf16)


def halve_body(keep_ref, recv_ref, kept_ref, send_ref):
    half = kept_ref.shape[0]
    kept_ref[...] = keep_ref[:half] + recv_ref[:half].astype(f32)
    send_ref[...] = (keep_ref[half:] + recv_ref[half:].astype(f32)).astype(bf16)


def halve_joined_body(keep_ref, recv_ref, rank_ref, rank_recv_ref, kept_ref, send_ref):
    half = keep_ref.shape[0] // 2
    kept_ref[:half] = keep_ref[:half] + recv_ref[:half].astype(f32)
    send_ref[:half] = (keep_ref[half:] + recv_ref[half:].astype(f32)).astype(bf16)
    rank = rank_ref[...] + rank_recv_ref[...]
    kept_ref[half:] = rank
    send_ref[half:] = rank.astype(bf16)


def halve_tail_body(keep_ref, recv_ref, kept_ref, send_ref):
    half = kept_ref.shape[0] - 2 * RANK
    kept_ref[:half] = keep_ref[:half] + recv_ref[:half].astype(f32)
    send_ref[:half] = (keep_ref[half : 2 * half] + recv_ref[half : 2 * half].astype(f32)).astype(bf16)
    total = keep_ref[2 * half :] + recv_ref[2 * half :].astype(f32)
    kept_ref[half:] = total
    send_ref[half:] = total.astype(bf16)


def halve(body, half, *args, **order):
    shape = (half, args[0].shape[1])
    return in_vmem(body, "halve", [(shape, f32), (shape, bf16)], *args, **order)


def hidden_body(
    gate_ref, gate_recv_ref, up_ref, up_recv_ref, gate_factor_ref, up_factor_ref, down_factor_ref, out_ref
):
    size = gate_factor_ref.shape[1]
    rank = (up_ref[size:] + up_recv_ref[size:].astype(f32)).astype(bf16)
    gate = lax.dot_general(
        gate_factor_ref[...], rank[:RANK], (((0,), (0,)), ((), ())), preferred_element_type=f32
    )
    gate = gate_ref[...] + gate_recv_ref[...].astype(f32) + adapter_scale * gate
    up = lax.dot_general(up_factor_ref[...], rank[RANK:], (((0,), (0,)), ((), ())), preferred_element_type=f32)
    up = up_ref[:size] + up_recv_ref[:size].astype(f32) + adapter_scale * up
    hidden = (gate / (1.0 + jnp.exp(-gate)) * up).astype(bf16)
    low = jnp.dot(down_factor_ref[...], hidden, preferred_element_type=f32).astype(bf16)
    for copy in range(out_ref.shape[0]):
        out_ref[copy, :size] = hidden
        out_ref[copy, size:] = low


def double_body(bit, mine_ref, theirs_ref, out_ref):
    count = mine_ref.shape[0]
    high = bit()
    out_ref[pl.ds(high * count, count)] = mine_ref[...]
    out_ref[pl.ds((1 - high) * count, count)] = theirs_ref[...]


def double_flat_body(bit, mine_ref, theirs_ref, out_ref):
    count, _, width = mine_ref.shape
    high = bit()
    for side, from_ref in ((high, mine_ref), (1 - high, theirs_ref)):
        for i in range(count):
            at = pl.multiple_of((side * count + i) * width, width)
            out_ref[:, pl.ds(at, width)] = from_ref[i]


def add_body(mine_ref, theirs_ref, out_ref):
    out_ref[...] = mine_ref[...] + theirs_ref[...]


def strip_body(from_ref, out_ref, low_ref):
    chips, size = from_ref.shape[0], from_ref.shape[1] - RANK
    low = jnp.zeros(low_ref.shape, f32)
    for chip in range(chips):
        out_ref[chip * size : (chip + 1) * size] = from_ref[chip, :size]
        low = low + from_ref[chip, size:].astype(f32)
    low_ref[...] = low


def down_rows_body(size, down_ref, own_ref, other_ref, token_ref, sem):
    core = lax.axis_index("c")
    token_ref[...] = jnp.zeros(token_ref.shape, f32)
    copies = []
    for side, to_ref in enumerate((own_ref, other_ref)):
        for chip in range(8):
            copies.append(
                pltpu.make_async_copy(
                    down_ref.at[rows_at(2 * chip + (core if side == 0 else 1 - core), size)],
                    to_ref.at[pl.ds(chip * size, size)],
                    sem.at[side * 8 + chip],
                )
            )
    for copy in copies:
        copy.start()
    for copy in copies:
        copy.wait()


def down_rows(size, down):
    units, width = down.shape
    half = jax.ShapeDtypeStruct((units // 2, width), down.dtype)
    whole = pl.BlockSpec(memory_space=pltpu.VMEM)
    return pl.pallas_call(
        functools.partial(down_rows_body, size),
        in_specs=[pl.BlockSpec(memory_space=pl.ANY)],
        out_specs=[whole] * 3,
        out_shape=[half, half, jax.ShapeDtypeStruct((8, 128), f32)],
        scratch_shapes=[pltpu.SemaphoreType.DMA((16,))],
        compiler_params=pltpu.CompilerParams(vmem_limit_bytes=VMEM_LIMIT),
        cost_estimate=pl.CostEstimate(flops=0, bytes_accessed=4 * units * width, transcendentals=0),
        name="down_rows",
    )(down)


def tp_blocks_body(own_ref, own_low_ref, other_ref, other_low_ref, factor_ref, out_ref):
    blocks, steps, block = out_ref.shape[:3]
    low = (own_low_ref[...] + other_low_ref[...]).astype(bf16)
    for s in range(steps):
        first = s * blocks * block
        rows = slice(first, first + blocks * block)
        term = lax.dot_general(
            low[:, rows], factor_ref[2 * RANK :], (((0,), (0,)), ((), ())), preferred_element_type=f32
        )
        total = (own_ref[rows] + other_ref[rows] + adapter_scale * term).astype(bf16)
        for t in range(blocks):
            out_ref[t, s] = total[t * block : (t + 1) * block]


def owner_sum_body(blocks_ref, out_ref):
    total = blocks_ref[0].astype(f32)
    for t in range(1, blocks_ref.shape[0]):
        total = total + blocks_ref[t].astype(f32)
    out_ref[...] = total.astype(bf16)


def per_device(
    normed,
    resident_gate_matrix,
    resident_up_matrix,
    resident_down_matrix,
    gate_input_factor,
    up_input_factor,
    gate_output_factor,
    up_output_factor,
    down_input_factor,
    down_output_factor,
):
    steps, rows, depth = normed.shape
    units = resident_gate_matrix.shape[1]
    size = units // 16
    lanes = steps * rows
    states = normed.reshape(lanes, depth)
    near, far, across = (
        functools.partial(ring_pair, "z", True),
        functools.partial(ring_pair, "z", False),
        functools.partial(swap, "yh"),
    )

    wide = jnp.concatenate([gate_input_factor, up_input_factor, down_output_factor.T], 0)[None]
    (wide,) = in_vmem(
        functools.partial(double_body, lambda: lax.axis_index("yl")),
        "double",
        [((2, *wide.shape[1:]), bf16)],
        wide,
        swap("yl", wide),
    )
    parts = [
        lax.dot_general(w, states, (((0,), (1,)), ((), ())), preferred_element_type=f32).astype(bf16)
        for w in (resident_gate_matrix, resident_up_matrix)
    ]
    recvs, sums, tokens = [], [], []
    for part, y_first in zip(parts, (True, False)):
        (send,) = in_vmem(
            functools.partial(other_core_body, size, y_first), "other_core", [((units // 2, lanes), bf16)], part
        )
        recvs.append(swap("c", send))
    for part, recv, y_first in zip(parts, recvs, (True, False)):
        shape = (4 * size, lanes)
        keep, send, token = in_vmem(
            functools.partial(core_sum_body, size, y_first),
            "core_sum",
            [(shape, f32), (shape, bf16)],
            part,
            recv,
            behind=tokens,
            token=True,
        )
        sums.append((keep, send))
        tokens = [token, wide]
    (wide,) = in_vmem(
        functools.partial(double_body, lambda: lax.axis_index("x") & 1),
        "double",
        [((4, *wide.shape[1:]), bf16)],
        wide,
        xor_pair("x", 1, wide),
    )
    (wide,) = in_vmem(
        functools.partial(double_flat_body, lambda: lax.axis_index("x") >> 1),
        "double",
        [((3 * RANK, depth), bf16)],
        wide,
        xor_pair("x", 3, wide),
    )
    rank = lax.dot_general(
        wide[: 2 * RANK], states, (((1,), (1,)), ((), ())), preferred_element_type=f32
    )
    (rank,) = in_vmem(add_body, "add", [(rank.shape, f32)], rank, swap("c", rank))

    *down, token = down_rows(size, resident_down_matrix)
    keep, send = sums[0]
    keep, send, crossed = halve(halve_body, 2 * size, keep, across(send), token=True)
    keep, send = halve(halve_body, size, keep, near(send))
    gate = keep, far(send)
    keep, send = sums[1]
    keep, send = halve(halve_joined_body, 2 * size + 2 * RANK, keep, near(send), rank, near(rank), behind=(crossed,))
    keep, send = halve(halve_tail_body, size + 2 * RANK, keep, far(send), behind=(token,))
    up = keep, across(send)
    (hidden,) = in_vmem(
        hidden_body,
        "hidden",
        [((8, size + RANK, lanes), bf16)],
        *gate,
        *up,
        gate_output_factor.T,
        up_output_factor.T,
        down_input_factor,
    )
    hidden = exchange(("yh", "z"), hidden)
    pieces = []
    for value, matrix in zip((hidden, swap("c", hidden)), down):
        value, low = in_vmem(
            strip_body, "strip", [((units // 2, lanes), bf16), ((RANK, lanes), f32)], value
        )
        part = lax.dot_general(value, matrix, (((0,), (0,)), ((), ())), preferred_element_type=f32)
        pieces += [part, low]
    (blocks,) = in_vmem(
        tp_blocks_body, "tp_blocks", [((8, steps, rows // 8, depth), bf16)], *pieces, wide
    )
    blocks = exchange(TP, blocks)
    return in_vmem(owner_sum_body, "owner_sum", [(blocks.shape[1:], bf16)], blocks)[0]


def solution(mesh):
    fine = Mesh(mesh.devices.reshape(2, 4, 2, 4, 2), FSDP + TP)
    fsdp, tp = FSDP, TP
    in_specs = (
        P(None, None, fsdp),
        P(fsdp, tp),
        P(fsdp, tp),
        P(tp, fsdp),
        P(None, fsdp + tp),
        P(None, fsdp + tp),
        P(tp + fsdp, None),
        P(tp + fsdp, None),
        P(None, tp + fsdp),
        P(fsdp + tp, None),
    )
    out_specs = P(None, tp, fsdp)
    return jax.shard_map(
        per_device, mesh=fine, in_specs=in_specs, out_specs=out_specs, check_vma=False
    )
```

profile of v0, /device:TPU:0, one launch (start us, length us, event | category | flops | bytes accessed | tf_op | source)
XLA Modules:
  0.0 116.1 jit_solution(10969989442215457516)
XLA Ops:
  0.0 0.0 copy-start
  0.0 1.2 %copy-done = bf16[2,256,1024]{2,1,0:T(8,128)(2,1)S(1)} copy-done((bf16[2,256,1024]{2,1,0:T(8,128)(2,1)S(1)}, bf16[2,256,1024]{2,1,0:T(8,128)(2,1)}, u32[]{:S(2)}) %copy-start) | copy-done | bytes 1048600
  1.2 0.0 copy-start.7
  1.2 7.1 %convolution_convert_fusion.1.refs_0_ = bf16[3328,512]{1,0:T(8,128)(2,1)S(1)} fusion(bf16[1024,3328]{1,0:T(8,128)(2,1)} %param.11, bf16[512,1024]{1,0:T(8,128)(2,1)S(1)} %bitcast.15), kind=kOutput, calls=%fused_computation.1 | convolution fusion | flops 3491364864 | bytes 11272192 | tf_op jit(solution)/shard_map/dot_general | solution.py:269
  8.3 0.1 other_core.2
  8.5 0.1 collective-permute-start
  8.5 0.0 copy-done.7
  8.6 4.1 %convolution_convert_fusion.refs_0_ = bf16[3328,512]{1,0:T(8,128)(2,1)S(1)} fusion(bf16[1024,3328]{1,0:T(8,128)(2,1)S(1)} %copy-done.7, bf16[512,1024]{1,0:T(8,128)(2,1)S(1)} %bitcast.16), kind=kOutput, calls=%fused_computation | convolution fusion | flops 3491364864 | bytes 11272192 | tf_op jit(solution)/shard_map/dot_general | solution.py:269
  12.7 0.0 copy-start.4
  12.7 0.0 copy-start.5
  12.7 0.0 copy-start.6
  12.8 0.1 other_core.3
  12.9 0.6 collective-permute-start.4
  13.4 0.0 copy-done.4
  13.4 0.0 copy-done.5
  13.4 0.0 copy-done.6
  13.5 1.7 %collective-permute-start.5 = (bf16[1,48,128]{2,1,0:T(8,128)(2,1)S(1)}, bf16[1,48,128]{2,1,0:T(8,128)(2,1)S(1)}, u32[]{:S(2)}, u32[]{:S(2)}) collective-permute-start(bf16[1,48,128]{2,1,0:T(8,128)(2,1)S(1)} %maximum_bitcast_fusion.refs_0_), channel_id=1, source_target_pairs={{0,1},{1,0},{2,3},{3,2},{4,5},{5,4},{6,7},{7,6},{8,9},{9,8},{10,11... | collective-permute-start | bytes 36872 | tf_op jit(solution)/shard_map/ppermute | solution.py:35
  15.2 2.0 %collective-permute-done.5.refs_1_ = bf16[1,48,128]{2,1,0:T(8,128)(2,1)S(1)} collective-permute-done((bf16[1,48,128]{2,1,0:T(8,128)(2,1)S(1)}, bf16[1,48,128]{2,1,0:T(8,128)(2,1)S(1)}, u32[]{:S(2)}, u32[]{:S(2)}) %collective-permute-start.5) | collective-permute-done | bytes 12320 | tf_op jit(solution)/shard_map/ppermute | solution.py:35
  17.2 0.0 collective-permute-done.refs_1_
  17.2 0.4 core_sum.2
  17.6 3.4 %collective-permute-start.1 = (bf16[832,512]{1,0:T(8,128)(2,1)S(1)}, bf16[832,512]{1,0:T(8,128)(2,1)S(1)}, u32[]{:S(2)}, u32[]{:S(2)}) collective-permute-start(bf16[832,512]{1,0:T(8,128)(2,1)S(1)} %get-tuple-element.27), channel_id=1, source_target_pairs={{0,64},{64,0},{1,65},{65,1},{2,66},{66,2},{3,67},{67,3},{4,68},{68... | collective-permute-start | bytes 2555912 | tf_op jit(solution)/shard_map/ppermute | solution.py:35
  21.0 0.0 collective-permute-done.4.refs_1_
  21.0 0.9 core_sum.3
  21.9 1.9 %collective-permute-start.6 = (bf16[832,512]{1,0:T(8,128)(2,1)S(1)}, bf16[832,512]{1,0:T(8,128)(2,1)S(1)}, u32[]{:S(2)}, u32[]{:S(2)}) collective-permute-start(bf16[832,512]{1,0:T(8,128)(2,1)S(1)} %get-tuple-element.34), channel_id=1, source_target_pairs={{0,16},{8,56},{16,0},{24,40},{32,48},{40,24},{48,32},{56,8},{1,17}... | collective-permute-start | bytes 2555912 | tf_op jit(solution)/shard_map/ppermute | solution.py:49
  23.8 1.5 %collective-permute-start.7 = (bf16[2,48,128]{2,1,0:T(8,128)(2,1)S(1)}, bf16[2,48,128]{2,1,0:T(8,128)(2,1)S(1)}, u32[]{:S(2)}, u32[]{:S(2)}) collective-permute-start(bf16[2,48,128]{2,1,0:T(8,128)(2,1)S(1)} %double.3.refs_3_.refs_0_), channel_id=1, source_target_pairs={{0,2},{2,0},{4,6},{6,4},{1,3},{3,1},{5,7},{7,5},{8,10},{10,8},{12,... | collective-permute-start | bytes 73736 | tf_op jit(solution)/shard_map/ppermute | solution.py:53
  25.3 2.5 %collective-permute-done.7.refs_1_ = bf16[2,48,128]{2,1,0:T(8,128)(2,1)S(1)} collective-permute-done((bf16[2,48,128]{2,1,0:T(8,128)(2,1)S(1)}, bf16[2,48,128]{2,1,0:T(8,128)(2,1)S(1)}, u32[]{:S(2)}, u32[]{:S(2)}) %collective-permute-start.7) | collective-permute-done | bytes 24608 | tf_op jit(solution)/shard_map/ppermute | solution.py:53
  27.8 2.8 %collective-permute-start.8 = (bf16[4,48,128]{2,1,0:T(8,128)(2,1)S(1)}, bf16[4,48,128]{2,1,0:T(8,128)(2,1)S(1)}, u32[]{:S(2)}, u32[]{:S(2)}) collective-permute-start(bf16[4,48,128]{2,1,0:T(8,128)(2,1)S(1)} %double.4.refs_0_), channel_id=1, source_target_pairs={{0,6},{2,4},{4,2},{6,0},{1,7},{3,5},{5,3},{7,1},{8,14},{10,12},{12... | collective-permute-start | bytes 147464 | tf_op jit(solution)/shard_map/ppermute | solution.py:53
  30.6 2.5 %collective-permute-done.8.refs_1_ = bf16[4,48,128]{2,1,0:T(8,128)(2,1)S(1)} collective-permute-done((bf16[4,48,128]{2,1,0:T(8,128)(2,1)S(1)}, bf16[4,48,128]{2,1,0:T(8,128)(2,1)S(1)}, u32[]{:S(2)}, u32[]{:S(2)}) %collective-permute-start.8) | collective-permute-done | bytes 49184 | tf_op jit(solution)/shard_map/ppermute | solution.py:53
  33.2 0.4 fusion.refs_0_
  33.6 0.0 collective-permute-start.9
  33.6 1.2 %collective-permute-done.9.refs_1_ = f32[32,512]{1,0:T(8,128)S(1)} collective-permute-done((f32[32,512]{1,0:T(8,128)S(1)}, f32[32,512]{1,0:T(8,128)S(1)}, u32[]{:S(2)}, u32[]{:S(2)}) %collective-permute-start.9) | collective-permute-done | bytes 65568 | tf_op jit(solution)/shard_map/ppermute | solution.py:35
  34.9 0.1 collective-permute-start.10
  35.0 4.4 %collective-permute-done.1.refs_1_ = bf16[832,512]{1,0:T(8,128)(2,1)S(1)} collective-permute-done((bf16[832,512]{1,0:T(8,128)(2,1)S(1)}, bf16[832,512]{1,0:T(8,128)(2,1)S(1)}, u32[]{:S(2)}, u32[]{:S(2)}) %collective-permute-start.1) | collective-permute-done | bytes 852000 | tf_op jit(solution)/shard_map/ppermute | solution.py:35
  39.4 0.2 halve.4
  39.6 0.0 collective-permute-done.10.refs_3_
  39.6 0.0 collective-permute-done.6.refs_1_
  39.6 0.1 halve.6
  39.8 4.2 %collective-permute-start.11 = (bf16[448,512]{1,0:T(8,128)(2,1)S(1)}, bf16[448,512]{1,0:T(8,128)(2,1)S(1)}, u32[]{:S(2)}, u32[]{:S(2)}) collective-permute-start(bf16[448,512]{1,0:T(8,128)(2,1)S(1)} %get-tuple-element.37), channel_id=1, source_target_pairs={{0,48},{8,24},{16,32},{24,8},{32,16},{40,56},{48,0},{56,40},{1,49}... | collective-permute-start | bytes 1376264 | tf_op jit(solution)/shard_map/ppermute | solution.py:49
  43.9 0.0 collective-permute-start.2
  43.9 0.0 slice-done
  43.9 0.0 slice-done.1
  44.0 3.9 %down_rows.1 = (bf16[1664,1024]{1,0:T(8,128)(2,1)S(1)}, bf16[1664,1024]{1,0:T(8,128)(2,1)S(1)}, f32[8,128]{1,0:T(8,128)S(1)}) custom-call(bf16[3328,1024]{1,0:T(8,128)(2,1)S(1)} %bitcast.19), custom_call_target="tpu_custom_call" | custom-call | bytes 13631488 | tf_op jit(solution)/shard_map/down_rows/pallas_call | solution.py:204
  47.8 5.6 %collective-permute-done.11.refs_1_ = bf16[448,512]{1,0:T(8,128)(2,1)S(1)} collective-permute-done((bf16[448,512]{1,0:T(8,128)(2,1)S(1)}, bf16[448,512]{1,0:T(8,128)(2,1)S(1)}, u32[]{:S(2)}, u32[]{:S(2)}) %collective-permute-start.11) | collective-permute-done | bytes 458784 | tf_op jit(solution)/shard_map/ppermute | solution.py:49
  53.4 0.1 halve.7
  53.5 3.1 %collective-permute-start.12 = (bf16[240,512]{1,0:T(8,128)(2,1)S(1)}, bf16[240,512]{1,0:T(8,128)(2,1)S(1)}, u32[]{:S(2)}, u32[]{:S(2)}) collective-permute-start(bf16[240,512]{1,0:T(8,128)(2,1)S(1)} %get-tuple-element.40), channel_id=1, source_target_pairs={{0,64},{64,0},{1,65},{65,1},{2,66},{66,2},{3,67},{67,3},{4,68},{68... | collective-permute-start | bytes 737288 | tf_op jit(solution)/shard_map/ppermute | solution.py:35
  56.6 0.0 collective-permute-done.2.refs_1_
  56.6 0.1 halve.5
  56.7 2.6 %collective-permute-start.3 = (bf16[208,512]{1,0:T(8,128)(2,1)S(1)}, bf16[208,512]{1,0:T(8,128)(2,1)S(1)}, u32[]{:S(2)}, u32[]{:S(2)}) collective-permute-start(bf16[208,512]{1,0:T(8,128)(2,1)S(1)} %get-tuple-element.31), channel_id=1, source_target_pairs={{0,48},{8,24},{16,32},{24,8},{32,16},{40,56},{48,0},{56,40},{1,49}... | collective-permute-start | bytes 638984 | tf_op jit(solution)/shard_map/ppermute | solution.py:49
  59.3 4.5 %collective-permute-done.3.refs_1_ = bf16[208,512]{1,0:T(8,128)(2,1)S(1)} collective-permute-done((bf16[208,512]{1,0:T(8,128)(2,1)S(1)}, bf16[208,512]{1,0:T(8,128)(2,1)S(1)}, u32[]{:S(2)}, u32[]{:S(2)}) %collective-permute-start.3) | collective-permute-done | bytes 213024 | tf_op jit(solution)/shard_map/ppermute | solution.py:49
  63.8 0.0 collective-permute-done.12.refs_3_
  63.8 0.0 copy-done.1
  63.8 0.0 copy-done.2
  63.8 0.0 copy-done.3
  63.8 0.6 hidden.1
  64.4 24.6 %all_to_all.10.refs_0_ = bf16[8,224,512]{2,1,0:T(8,128)(2,1)S(1)} all-to-all(bf16[8,224,512]{2,1,0:T(8,128)(2,1)S(1)} %hidden.1), channel_id=1, replica_groups=mesh['yh'=2,'z'=4,'c'=2,'x'=4,'yl'=2] {'yh','z'}, dimensions={0} | all-to-all | bytes 3670016 | tf_op jit(solution)/shard_map/all_to_all | solution.py:57
  89.0 0.0 collective-permute-start.13
  89.0 0.1 strip.2
  89.1 2.1 %fusion.2.refs_0_ = f32[512,1024]{1,0:T(8,128)S(1)} fusion(bf16[1664,512]{1,0:T(8,128)(2,1)S(1)} %get-tuple-element.41, bf16[1664,1024]{1,0:T(8,128)(2,1)S(1)} %get-tuple-element.42), kind=kOutput, calls=%fused_computation.5 | convolution fusion | flops 1744830464 | bytes 7208960 | tf_op jit(solution)/shard_map/dot_general | solution.py:335
  91.2 1.6 %collective-permute-done.13.refs_0_ = bf16[8,224,512]{2,1,0:T(8,128)(2,1)S(1)} collective-permute-done((bf16[8,224,512]{2,1,0:T(8,128)(2,1)S(1)}, bf16[8,224,512]{2,1,0:T(8,128)(2,1)S(1)}, u32[]{:S(2)}, u32[]{:S(2)}) %collective-permute-start.13) | collective-permute-done | bytes 1835040 | tf_op jit(solution)/shard_map/ppermute | solution.py:35
  92.8 0.1 strip.3
  92.9 2.1 %fusion.3.refs_2_ = f32[512,1024]{1,0:T(8,128)S(1)} fusion(bf16[1664,512]{1,0:T(8,128)(2,1)S(1)} %get-tuple-element.44, bf16[1664,1024]{1,0:T(8,128)(2,1)S(1)} %get-tuple-element.45), kind=kOutput, calls=%fused_computation.6 | convolution fusion | flops 1744830464 | bytes 7208960 | tf_op jit(solution)/shard_map/dot_general | solution.py:335
  95.0 0.5 tp_blocks.1
  95.4 19.9 %all_to_all.11.refs_0_ = bf16[8,2,32,1024]{3,2,1,0:T(8,128)(2,1)S(1)} all-to-all(bf16[8,2,32,1024]{3,2,1,0:T(8,128)(2,1)S(1)} %tp_blocks.1), channel_id=1, replica_groups=mesh['yh'=2,'z'=4,'c'=2,'x'=4,'yl'=2] {'x','yl'}, dimensions={0} | all-to-all | bytes 2097152 | tf_op jit(solution)/shard_map/all_to_all | solution.py:57
  115.3 0.8 owner_sum.1
  (11 shorter events, 0.1 us)
Async XLA Ops:
  0.0 1.2 %copy-start = (bf16[2,256,1024]{2,1,0:T(8,128)(2,1)S(1)}, bf16[2,256,1024]{2,1,0:T(8,128)(2,1)}, u32[]{:S(2)}) copy-start(bf16[2,256,1024]{2,1,0:T(8,128)(2,1)} %param.10) | copy-start | bytes 3145732
  1.2 7.3 %copy-start.7 = (bf16[1024,3328]{1,0:T(8,128)(2,1)S(1)}, bf16[1024,3328]{1,0:T(8,128)(2,1)}, u32[]{:S(2)}) copy-start(bf16[1024,3328]{1,0:T(8,128)(2,1)} %param.12) | copy-start | bytes 20447236
  8.5 8.8 %collective-permute-start = (bf16[1664,512]{1,0:T(8,128)(2,1)S(1)}, bf16[1664,512]{1,0:T(8,128)(2,1)S(1)}, u32[]{:S(2)}, u32[]{:S(2)}) collective-permute-start(bf16[1664,512]{1,0:T(8,128)(2,1)S(1)} %other_core.2), channel_id=1, source_target_pairs={{0,8},{8,0},{1,9},{9,1},{2,10},{10,2},{3,11},{11,3},{4,12},{12,4},... | collective-permute-start | bytes 5111816 | tf_op jit(solution)/shard_map/ppermute | solution.py:35
  12.7 0.7 copy-start.4
  12.7 0.7 copy-start.5
  12.7 0.7 copy-start.6
  12.9 8.1 %collective-permute-start.4 = (bf16[1664,512]{1,0:T(8,128)(2,1)S(1)}, bf16[1664,512]{1,0:T(8,128)(2,1)S(1)}, u32[]{:S(2)}, u32[]{:S(2)}) collective-permute-start(bf16[1664,512]{1,0:T(8,128)(2,1)S(1)} %other_core.3), channel_id=1, source_target_pairs={{0,8},{8,0},{1,9},{9,1},{2,10},{10,2},{3,11},{11,3},{4,12},{12,4},... | collective-permute-start | bytes 5111816 | tf_op jit(solution)/shard_map/ppermute | solution.py:35
  13.5 3.8 %collective-permute-start.5 = (bf16[1,48,128]{2,1,0:T(8,128)(2,1)S(1)}, bf16[1,48,128]{2,1,0:T(8,128)(2,1)S(1)}, u32[]{:S(2)}, u32[]{:S(2)}) collective-permute-start(bf16[1,48,128]{2,1,0:T(8,128)(2,1)S(1)} %maximum_bitcast_fusion.refs_0_), channel_id=1, source_target_pairs={{0,1},{1,0},{2,3},{3,2},{4,5},{5,4},{6,7},{7,6},{8,9},{9,8},{10,11... | collective-permute-start | bytes 36872 | tf_op jit(solution)/shard_map/ppermute | solution.py:35
  17.2 26.7 %slice-start = ((s8[6815744]{0:T(1024)(128)(4,1)}), s8[2621440]{0:T(1024)(128)(4,1)S(1)}, s32[]{:S(2)}) async-start(s8[6815744]{0:T(1024)(128)(4,1)} %bitcast.18), calls=%async_computation.2 | async-start | bytes 5242880
  17.6 21.8 %collective-permute-start.1 = (bf16[832,512]{1,0:T(8,128)(2,1)S(1)}, bf16[832,512]{1,0:T(8,128)(2,1)S(1)}, u32[]{:S(2)}, u32[]{:S(2)}) collective-permute-start(bf16[832,512]{1,0:T(8,128)(2,1)S(1)} %get-tuple-element.27), channel_id=1, source_target_pairs={{0,64},{64,0},{1,65},{65,1},{2,66},{66,2},{3,67},{67,3},{4,68},{68... | collective-permute-start | bytes 2555912 | tf_op jit(solution)/shard_map/ppermute | solution.py:35
  21.0 23.0 %slice-start.1 = ((s8[6815744]{0:T(1024)(128)(4,1)}), s8[4194304]{0:T(1024)(128)(4,1)S(1)}, s32[]{:S(2)}) async-start(s8[6815744]{0:T(1024)(128)(4,1)} %bitcast.18), calls=%async_computation.3 | async-start | bytes 8388608
  21.9 17.7 %collective-permute-start.6 = (bf16[832,512]{1,0:T(8,128)(2,1)S(1)}, bf16[832,512]{1,0:T(8,128)(2,1)S(1)}, u32[]{:S(2)}, u32[]{:S(2)}) collective-permute-start(bf16[832,512]{1,0:T(8,128)(2,1)S(1)} %get-tuple-element.34), channel_id=1, source_target_pairs={{0,16},{8,56},{16,0},{24,40},{32,48},{40,24},{48,32},{56,8},{1,17}... | collective-permute-start | bytes 2555912 | tf_op jit(solution)/shard_map/ppermute | solution.py:49
  23.8 4.0 %collective-permute-start.7 = (bf16[2,48,128]{2,1,0:T(8,128)(2,1)S(1)}, bf16[2,48,128]{2,1,0:T(8,128)(2,1)S(1)}, u32[]{:S(2)}, u32[]{:S(2)}) collective-permute-start(bf16[2,48,128]{2,1,0:T(8,128)(2,1)S(1)} %double.3.refs_3_.refs_0_), channel_id=1, source_target_pairs={{0,2},{2,0},{4,6},{6,4},{1,3},{3,1},{5,7},{7,5},{8,10},{10,8},{12,... | collective-permute-start | bytes 73736 | tf_op jit(solution)/shard_map/ppermute | solution.py:53
  27.8 5.3 %collective-permute-start.8 = (bf16[4,48,128]{2,1,0:T(8,128)(2,1)S(1)}, bf16[4,48,128]{2,1,0:T(8,128)(2,1)S(1)}, u32[]{:S(2)}, u32[]{:S(2)}) collective-permute-start(bf16[4,48,128]{2,1,0:T(8,128)(2,1)S(1)} %double.4.refs_0_), channel_id=1, source_target_pairs={{0,6},{2,4},{4,2},{6,0},{1,7},{3,5},{5,3},{7,1},{8,14},{10,12},{12... | collective-permute-start | bytes 147464 | tf_op jit(solution)/shard_map/ppermute | solution.py:53
  33.6 1.3 %collective-permute-start.9 = (f32[32,512]{1,0:T(8,128)S(1)}, f32[32,512]{1,0:T(8,128)S(1)}, u32[]{:S(2)}, u32[]{:S(2)}) collective-permute-start(f32[32,512]{1,0:T(8,128)S(1)} %fusion.refs_0_), channel_id=1, source_target_pairs={{0,8},{8,0},{1,9},{9,1},{2,10},{10,2},{3,11},{11,3},{4,12},{12,4},... | collective-permute-start | bytes 196616 | tf_op jit(solution)/shard_map/ppermute | solution.py:35
  34.9 4.7 %collective-permute-start.10 = (f32[32,512]{1,0:T(8,128)S(1)}, f32[32,512]{1,0:T(8,128)S(1)}, u32[]{:S(2)}, u32[]{:S(2)}) collective-permute-start(f32[32,512]{1,0:T(8,128)S(1)} %add.1.refs_2_), channel_id=1, source_target_pairs={{0,16},{8,56},{16,0},{24,40},{32,48},{40,24},{48,32},{56,8},{1,17}... | collective-permute-start | bytes 196616 | tf_op jit(solution)/shard_map/ppermute | solution.py:49
  39.8 13.6 %collective-permute-start.11 = (bf16[448,512]{1,0:T(8,128)(2,1)S(1)}, bf16[448,512]{1,0:T(8,128)(2,1)S(1)}, u32[]{:S(2)}, u32[]{:S(2)}) collective-permute-start(bf16[448,512]{1,0:T(8,128)(2,1)S(1)} %get-tuple-element.37), channel_id=1, source_target_pairs={{0,48},{8,24},{16,32},{24,8},{32,16},{40,56},{48,0},{56,40},{1,49}... | collective-permute-start | bytes 1376264 | tf_op jit(solution)/shard_map/ppermute | solution.py:49
  43.9 19.9 %copy-start.1 = (bf16[208,16]{0,1:T(8,128)(2,1)S(1)}, bf16[208,16]{0,1:T(8,128)(2,1)}, u32[]{:S(2)}) copy-start(bf16[208,16]{0,1:T(8,128)(2,1)} %param.16) | copy-start | bytes 19972
  43.9 19.9 %copy-start.2 = (bf16[208,16]{0,1:T(8,128)(2,1)S(1)}, bf16[208,16]{0,1:T(8,128)(2,1)}, u32[]{:S(2)}) copy-start(bf16[208,16]{0,1:T(8,128)(2,1)} %param.17) | copy-start | bytes 19972
  43.9 19.9 %copy-start.3 = (bf16[16,208]{1,0:T(8,128)(2,1)S(1)}, bf16[16,208]{1,0:T(8,128)(2,1)}, u32[]{:S(2)}) copy-start(bf16[16,208]{1,0:T(8,128)(2,1)} %refs_6_.1) | copy-start | bytes 19972
  43.9 12.6 %collective-permute-start.2 = (bf16[416,512]{1,0:T(8,128)(2,1)S(1)}, bf16[416,512]{1,0:T(8,128)(2,1)S(1)}, u32[]{:S(2)}, u32[]{:S(2)}) collective-permute-start(bf16[416,512]{1,0:T(8,128)(2,1)S(1)} %get-tuple-element.29), channel_id=1, source_target_pairs={{0,16},{8,56},{16,0},{24,40},{32,48},{40,24},{48,32},{56,8},{1,17}... | collective-permute-start | bytes 1277960 | tf_op jit(solution)/shard_map/ppermute | solution.py:49
  53.5 10.3 %collective-permute-start.12 = (bf16[240,512]{1,0:T(8,128)(2,1)S(1)}, bf16[240,512]{1,0:T(8,128)(2,1)S(1)}, u32[]{:S(2)}, u32[]{:S(2)}) collective-permute-start(bf16[240,512]{1,0:T(8,128)(2,1)S(1)} %get-tuple-element.40), channel_id=1, source_target_pairs={{0,64},{64,0},{1,65},{65,1},{2,66},{66,2},{3,67},{67,3},{4,68},{68... | collective-permute-start | bytes 737288 | tf_op jit(solution)/shard_map/ppermute | solution.py:35
  56.7 7.1 %collective-permute-start.3 = (bf16[208,512]{1,0:T(8,128)(2,1)S(1)}, bf16[208,512]{1,0:T(8,128)(2,1)S(1)}, u32[]{:S(2)}, u32[]{:S(2)}) collective-permute-start(bf16[208,512]{1,0:T(8,128)(2,1)S(1)} %get-tuple-element.31), channel_id=1, source_target_pairs={{0,48},{8,24},{16,32},{24,8},{32,16},{40,56},{48,0},{56,40},{1,49}... | collective-permute-start | bytes 638984 | tf_op jit(solution)/shard_map/ppermute | solution.py:49
  89.0 3.8 %collective-permute-start.13 = (bf16[8,224,512]{2,1,0:T(8,128)(2,1)S(1)}, bf16[8,224,512]{2,1,0:T(8,128)(2,1)S(1)}, u32[]{:S(2)}, u32[]{:S(2)}) collective-permute-start(bf16[8,224,512]{2,1,0:T(8,128)(2,1)S(1)} %all_to_all.10.refs_0_), channel_id=1, source_target_pairs={{0,8},{8,0},{1,9},{9,1},{2,10},{10,2},{3,11},{11,3},{4,12},{12,4},... | collective-permute-start | bytes 5505032 | tf_op jit(solution)/shard_map/ppermute | solution.py:35
where the time goes:
time: 116 us
  blocking collectives  44.4 us (38%)
  waiting for transfers between devices  24.4 us (21%)
  starting transfers between devices  21.9 us (19%)
  matrix products  15.8 us (14%)
  Pallas kernels  8.08 us (7%)
  local copies, waits for them, and re-layouts  1.27 us (1%)
    all_to_all x2, blocking collectives, exchange(): return lax.all_to_all(value, axes, split_axis=0, concat_axis=0)  44.4 us
    dot_general x2, matrix products, per_device(): lax.dot_general(w, states, (((0,), (1,)), ((), ())), preferred_element_ty...  11.2 us
    ppermute x5, waiting for transfers between devices, ring_pair(): return lax.ppermute(value, axes, moves)  10.1 us
    ppermute x7, waiting for transfers between devices, swap(): return lax.ppermute(value, axis, [(0, 1), (1, 0)])  9.31 us
    ppermute x7, starting transfers between devices, swap(): return lax.ppermute(value, axis, [(0, 1), (1, 0)])  8.81 us
    ppermute x5, starting transfers between devices, ring_pair(): return lax.ppermute(value, axes, moves)  8.78 us
    ppermute x2, waiting for transfers between devices, xor_pair(): return lax.ppermute(value, axis, [(i, i ^ step) for i in range(4)])  5.02 us
    ppermute x2, starting transfers between devices, xor_pair(): return lax.ppermute(value, axis, [(i, i ^ step) for i in range(4)])  4.26 us
  transfers between devices with their start and end apart: 14, of which 8 were waited for; matrix products, arithmetic and copies ran while one was open for 6% of the time, Pallas kernels for 5%

commit v1 on v0

--- a/solution.py
+++ b/solution.py
@@ -272,7 +272,7 @@
     recvs, sums, tokens = [], [], []
     for part, y_first in zip(parts, (True, False)):
         (send,) = in_vmem(
-            functools.partial(other_core_body, size, y_first), "other_core", [((units // 2, lanes), bf16)], part
+            functools.partial(other_core_body, size, y_first), "other_core", [((units // 2, lanes), bf16)], part, behind=() if y_first else (wide,)
         )
         recvs.append(swap("c", send))
     for part, recv, y_first in zip(parts, recvs, (True, False)):

time: 116 us -> 116 us (level)
  local copies, waits for them, and re-layouts: 1.27 us -> 0.03 us
    ppermute x7, waiting for transfers between devices: 9.31 us -> 7.65 us  [swap(): return lax.ppermute(value, axis, [(0, 1), (1, 0)])]
    unnamed x20 -> x14, local copies, waits for them, and re-layouts: 1.27 us -> 0.03 us
  transfers between devices with their start and end apart: 14 -> 14, of which waited for: 8 -> 7; matrix products, arithmetic and copies ran while one was open for 6% -> 12% of each run, Pallas kernels for 5% -> 5%
where the time goes in v1:
time: 116 us
  blocking collectives  45.2 us (39%)
  waiting for transfers between devices  23.5 us (20%)
  starting transfers between devices  21.9 us (19%)
  matrix products  15.8 us (14%)
  Pallas kernels  8.02 us (7%)
    all_to_all x2, blocking collectives, exchange(): return lax.all_to_all(value, axes, split_axis=0, concat_axis=0)  45.2 us
    dot_general x2, matrix products, per_device(): lax.dot_general(w, states, (((0,), (1,)), ((), ())), preferred_element_ty...  11.2 us
    ppermute x5, waiting for transfers between devices, ring_pair(): return lax.ppermute(value, axes, moves)  10.7 us
    ppermute x5, starting transfers between devices, ring_pair(): return lax.ppermute(value, axes, moves)  9.02 us
    ppermute x7, starting transfers between devices, swap(): return lax.ppermute(value, axis, [(0, 1), (1, 0)])  8.64 us
    ppermute x7, waiting for transfers between devices, swap(): return lax.ppermute(value, axis, [(0, 1), (1, 0)])  7.65 us
    ppermute x2, waiting for transfers between devices, xor_pair(): return lax.ppermute(value, axis, [(i, i ^ step) for i in range(4)])  5.15 us
    ppermute x2, starting transfers between devices, xor_pair(): return lax.ppermute(value, axis, [(i, i ^ step) for i in range(4)])  4.26 us
  transfers between devices with their start and end apart: 14, of which 7 were waited for; matrix products, arithmetic and copies ran while one was open for 12% of the time, Pallas kernels for 5%

profile of v1, /device:TPU:0, one launch (start us, length us, event | category | flops | bytes accessed | tf_op | source)
XLA Modules:
  0.0 115.5 jit_solution(10906649632450400325)
XLA Ops:
  0.0 0.0 copy-start
  0.0 0.8 maximum_bitcast_fusion.refs_0_
  0.8 1.7 %collective-permute-start.4 = (bf16[1,48,128]{2,1,0:T(8,128)(2,1)S(1)}, bf16[1,48,128]{2,1,0:T(8,128)(2,1)S(1)}, u32[]{:S(2)}, u32[]{:S(2)}) collective-permute-start(bf16[1,48,128]{2,1,0:T(8,128)(2,1)S(1)} %maximum_bitcast_fusion.refs_0_), channel_id=1, source_target_pairs={{0,1},{1,0},{2,3},{3,2},{4,5},{5,4},{6,7},{7,6},{8,9},{9,8},{10,11... | collective-permute-start | bytes 36872 | tf_op jit(solution)/shard_map/ppermute | solution.py:35
  2.5 0.0 copy-done
  2.5 0.0 copy-start.4
  2.5 7.1 %convolution_convert_fusion.1.refs_0_ = bf16[3328,512]{1,0:T(8,128)(2,1)S(1)} fusion(bf16[1024,3328]{1,0:T(8,128)(2,1)} %param.11, bf16[512,1024]{1,0:T(8,128)(2,1)S(1)} %bitcast.15), kind=kOutput, calls=%fused_computation.1 | convolution fusion | flops 3491364864 | bytes 11272192 | tf_op jit(solution)/shard_map/dot_general | solution.py:269
  9.6 0.1 other_core.2
  9.7 0.1 collective-permute-start
  9.8 0.0 copy-done.4
  9.8 4.1 %convolution_convert_fusion.refs_0_ = bf16[3328,512]{1,0:T(8,128)(2,1)S(1)} fusion(bf16[1024,3328]{1,0:T(8,128)(2,1)S(1)} %copy-done.4, bf16[512,1024]{1,0:T(8,128)(2,1)S(1)} %bitcast.16), kind=kOutput, calls=%fused_computation | convolution fusion | flops 3491364864 | bytes 11272192 | tf_op jit(solution)/shard_map/dot_general | solution.py:269
  14.0 0.0 collective-permute-done.4.refs_1_
  14.0 0.1 other_core.3
  14.1 0.6 collective-permute-start.5
  14.7 0.0 collective-permute-done.refs_1_
  14.7 0.0 slice-start
  14.7 0.4 core_sum.2
  15.1 3.0 %collective-permute-start.1 = (bf16[832,512]{1,0:T(8,128)(2,1)S(1)}, bf16[832,512]{1,0:T(8,128)(2,1)S(1)}, u32[]{:S(2)}, u32[]{:S(2)}) collective-permute-start(bf16[832,512]{1,0:T(8,128)(2,1)S(1)} %get-tuple-element.27), channel_id=1, source_target_pairs={{0,64},{64,0},{1,65},{65,1},{2,66},{66,2},{3,67},{67,3},{4,68},{68... | collective-permute-start | bytes 2555912 | tf_op jit(solution)/shard_map/ppermute | solution.py:35
  18.0 0.0 collective-permute-done.5.refs_1_
  18.1 0.0 slice-start.1
  18.1 0.9 core_sum.3
  18.9 1.9 %collective-permute-start.6 = (bf16[832,512]{1,0:T(8,128)(2,1)S(1)}, bf16[832,512]{1,0:T(8,128)(2,1)S(1)}, u32[]{:S(2)}, u32[]{:S(2)}) collective-permute-start(bf16[832,512]{1,0:T(8,128)(2,1)S(1)} %get-tuple-element.34), channel_id=1, source_target_pairs={{0,16},{8,56},{16,0},{24,40},{32,48},{40,24},{48,32},{56,8},{1,17}... | collective-permute-start | bytes 2555912 | tf_op jit(solution)/shard_map/ppermute | solution.py:49
  20.8 1.5 %collective-permute-start.7 = (bf16[2,48,128]{2,1,0:T(8,128)(2,1)S(1)}, bf16[2,48,128]{2,1,0:T(8,128)(2,1)S(1)}, u32[]{:S(2)}, u32[]{:S(2)}) collective-permute-start(bf16[2,48,128]{2,1,0:T(8,128)(2,1)S(1)} %double.3.refs_1_.refs_3_.refs_0_), channel_id=1, source_target_pairs={{0,2},{2,0},{4,6},{6,4},{1,3},{3,1},{5,7},{7,5},{8,10},{10,8},{12,... | collective-permute-start | bytes 73736 | tf_op jit(solution)/shard_map/ppermute | solution.py:53
  22.3 2.3 %collective-permute-done.7.refs_1_ = bf16[2,48,128]{2,1,0:T(8,128)(2,1)S(1)} collective-permute-done((bf16[2,48,128]{2,1,0:T(8,128)(2,1)S(1)}, bf16[2,48,128]{2,1,0:T(8,128)(2,1)S(1)}, u32[]{:S(2)}, u32[]{:S(2)}) %collective-permute-start.7) | collective-permute-done | bytes 24608 | tf_op jit(solution)/shard_map/ppermute | solution.py:53
  24.7 2.8 %collective-permute-start.8 = (bf16[4,48,128]{2,1,0:T(8,128)(2,1)S(1)}, bf16[4,48,128]{2,1,0:T(8,128)(2,1)S(1)}, u32[]{:S(2)}, u32[]{:S(2)}) collective-permute-start(bf16[4,48,128]{2,1,0:T(8,128)(2,1)S(1)} %double.4.refs_0_), channel_id=1, source_target_pairs={{0,6},{2,4},{4,2},{6,0},{1,7},{3,5},{5,3},{7,1},{8,14},{10,12},{12... | collective-permute-start | bytes 147464 | tf_op jit(solution)/shard_map/ppermute | solution.py:53
  27.4 2.8 %collective-permute-done.8.refs_1_ = bf16[4,48,128]{2,1,0:T(8,128)(2,1)S(1)} collective-permute-done((bf16[4,48,128]{2,1,0:T(8,128)(2,1)S(1)}, bf16[4,48,128]{2,1,0:T(8,128)(2,1)S(1)}, u32[]{:S(2)}, u32[]{:S(2)}) %collective-permute-start.8) | collective-permute-done | bytes 49184 | tf_op jit(solution)/shard_map/ppermute | solution.py:53
  30.3 0.4 fusion.refs_0_
  30.7 0.4 collective-permute-start.9
  31.1 0.9 collective-permute-done.9.refs_1_
  32.0 0.4 collective-permute-start.10
  32.4 5.2 %collective-permute-done.1.refs_1_ = bf16[832,512]{1,0:T(8,128)(2,1)S(1)} collective-permute-done((bf16[832,512]{1,0:T(8,128)(2,1)S(1)}, bf16[832,512]{1,0:T(8,128)(2,1)S(1)}, u32[]{:S(2)}, u32[]{:S(2)}) %collective-permute-start.1) | collective-permute-done | bytes 852000 | tf_op jit(solution)/shard_map/ppermute | solution.py:35
  37.5 0.2 halve.4
  37.7 0.0 collective-permute-done.10.refs_3_
  37.7 0.0 collective-permute-done.6.refs_1_
  37.8 0.1 halve.6
  37.9 4.1 %collective-permute-start.11 = (bf16[448,512]{1,0:T(8,128)(2,1)S(1)}, bf16[448,512]{1,0:T(8,128)(2,1)S(1)}, u32[]{:S(2)}, u32[]{:S(2)}) collective-permute-start(bf16[448,512]{1,0:T(8,128)(2,1)S(1)} %get-tuple-element.37), channel_id=1, source_target_pairs={{0,48},{8,24},{16,32},{24,8},{32,16},{40,56},{48,0},{56,40},{1,49}... | collective-permute-start | bytes 1376264 | tf_op jit(solution)/shard_map/ppermute | solution.py:49
  42.0 0.0 copy-start.1
  42.0 0.0 copy-start.2
  42.0 0.0 copy-start.3
  42.0 0.0 collective-permute-start.2
  42.0 0.0 slice-done
  42.0 0.0 slice-done.1
  42.1 3.9 %down_rows.1 = (bf16[1664,1024]{1,0:T(8,128)(2,1)S(1)}, bf16[1664,1024]{1,0:T(8,128)(2,1)S(1)}, f32[8,128]{1,0:T(8,128)S(1)}) custom-call(bf16[3328,1024]{1,0:T(8,128)(2,1)S(1)} %bitcast.19), custom_call_target="tpu_custom_call" | custom-call | bytes 13631488 | tf_op jit(solution)/shard_map/down_rows/pallas_call | solution.py:204
  45.9 6.2 %collective-permute-done.11.refs_1_ = bf16[448,512]{1,0:T(8,128)(2,1)S(1)} collective-permute-done((bf16[448,512]{1,0:T(8,128)(2,1)S(1)}, bf16[448,512]{1,0:T(8,128)(2,1)S(1)}, u32[]{:S(2)}, u32[]{:S(2)}) %collective-permute-start.11) | collective-permute-done | bytes 458784 | tf_op jit(solution)/shard_map/ppermute | solution.py:49
  52.1 0.1 halve.7
  52.2 3.0 %collective-permute-start.12 = (bf16[240,512]{1,0:T(8,128)(2,1)S(1)}, bf16[240,512]{1,0:T(8,128)(2,1)S(1)}, u32[]{:S(2)}, u32[]{:S(2)}) collective-permute-start(bf16[240,512]{1,0:T(8,128)(2,1)S(1)} %get-tuple-element.40), channel_id=1, source_target_pairs={{0,64},{64,0},{1,65},{65,1},{2,66},{66,2},{3,67},{67,3},{4,68},{68... | collective-permute-start | bytes 737288 | tf_op jit(solution)/shard_map/ppermute | solution.py:35
  55.2 0.0 collective-permute-done.2.refs_1_
  55.2 0.1 halve.5
  55.3 2.6 %collective-permute-start.3 = (bf16[208,512]{1,0:T(8,128)(2,1)S(1)}, bf16[208,512]{1,0:T(8,128)(2,1)S(1)}, u32[]{:S(2)}, u32[]{:S(2)}) collective-permute-start(bf16[208,512]{1,0:T(8,128)(2,1)S(1)} %get-tuple-element.31), channel_id=1, source_target_pairs={{0,48},{8,24},{16,32},{24,8},{32,16},{40,56},{48,0},{56,40},{1,49}... | collective-permute-start | bytes 638984 | tf_op jit(solution)/shard_map/ppermute | solution.py:49
  57.9 4.5 %collective-permute-done.3.refs_1_ = bf16[208,512]{1,0:T(8,128)(2,1)S(1)} collective-permute-done((bf16[208,512]{1,0:T(8,128)(2,1)S(1)}, bf16[208,512]{1,0:T(8,128)(2,1)S(1)}, u32[]{:S(2)}, u32[]{:S(2)}) %collective-permute-start.3) | collective-permute-done | bytes 213024 | tf_op jit(solution)/shard_map/ppermute | solution.py:49
  62.4 0.0 collective-permute-done.12.refs_3_
  62.4 0.0 copy-done.1
  62.4 0.0 copy-done.2
  62.4 0.0 copy-done.3
  62.4 0.6 hidden.1
  63.0 25.5 %all_to_all.10.refs_0_ = bf16[8,224,512]{2,1,0:T(8,128)(2,1)S(1)} all-to-all(bf16[8,224,512]{2,1,0:T(8,128)(2,1)S(1)} %hidden.1), channel_id=1, replica_groups=mesh['yh'=2,'z'=4,'c'=2,'x'=4,'yl'=2] {'yh','z'}, dimensions={0} | all-to-all | bytes 3670016 | tf_op jit(solution)/shard_map/all_to_all | solution.py:57
  88.5 0.0 collective-permute-start.13
  88.5 0.1 strip.2
  88.7 2.1 %fusion.2.refs_0_ = f32[512,1024]{1,0:T(8,128)S(1)} fusion(bf16[1664,512]{1,0:T(8,128)(2,1)S(1)} %get-tuple-element.41, bf16[1664,1024]{1,0:T(8,128)(2,1)S(1)} %get-tuple-element.42), kind=kOutput, calls=%fused_computation.5 | convolution fusion | flops 1744830464 | bytes 7208960 | tf_op jit(solution)/shard_map/dot_general | solution.py:335
  90.7 1.6 %collective-permute-done.13.refs_0_ = bf16[8,224,512]{2,1,0:T(8,128)(2,1)S(1)} collective-permute-done((bf16[8,224,512]{2,1,0:T(8,128)(2,1)S(1)}, bf16[8,224,512]{2,1,0:T(8,128)(2,1)S(1)}, u32[]{:S(2)}, u32[]{:S(2)}) %collective-permute-start.13) | collective-permute-done | bytes 1835040 | tf_op jit(solution)/shard_map/ppermute | solution.py:35
  92.3 0.1 strip.3
  92.4 2.1 %fusion.3.refs_2_ = f32[512,1024]{1,0:T(8,128)S(1)} fusion(bf16[1664,512]{1,0:T(8,128)(2,1)S(1)} %get-tuple-element.44, bf16[1664,1024]{1,0:T(8,128)(2,1)S(1)} %get-tuple-element.45), kind=kOutput, calls=%fused_computation.6 | convolution fusion | flops 1744830464 | bytes 7208960 | tf_op jit(solution)/shard_map/dot_general | solution.py:335
  94.5 0.5 tp_blocks.1
  95.0 19.7 %all_to_all.11.refs_0_ = bf16[8,2,32,1024]{3,2,1,0:T(8,128)(2,1)S(1)} all-to-all(bf16[8,2,32,1024]{3,2,1,0:T(8,128)(2,1)S(1)} %tp_blocks.1), channel_id=1, replica_groups=mesh['yh'=2,'z'=4,'c'=2,'x'=4,'yl'=2] {'x','yl'}, dimensions={0} | all-to-all | bytes 2097152 | tf_op jit(solution)/shard_map/all_to_all | solution.py:57
  114.7 0.8 owner_sum.1
  (5 shorter events, 0.1 us)
Async XLA Ops:
  0.0 2.5 %copy-start = (bf16[2,256,1024]{2,1,0:T(8,128)(2,1)S(1)}, bf16[2,256,1024]{2,1,0:T(8,128)(2,1)}, u32[]{:S(2)}) copy-start(bf16[2,256,1024]{2,1,0:T(8,128)(2,1)} %param.10) | copy-start | bytes 3145732
  0.8 13.2 %collective-permute-start.4 = (bf16[1,48,128]{2,1,0:T(8,128)(2,1)S(1)}, bf16[1,48,128]{2,1,0:T(8,128)(2,1)S(1)}, u32[]{:S(2)}, u32[]{:S(2)}) collective-permute-start(bf16[1,48,128]{2,1,0:T(8,128)(2,1)S(1)} %maximum_bitcast_fusion.refs_0_), channel_id=1, source_target_pairs={{0,1},{1,0},{2,3},{3,2},{4,5},{5,4},{6,7},{7,6},{8,9},{9,8},{10,11... | collective-permute-start | bytes 36872 | tf_op jit(solution)/shard_map/ppermute | solution.py:35
  2.5 7.3 %copy-start.4 = (bf16[1024,3328]{1,0:T(8,128)(2,1)S(1)}, bf16[1024,3328]{1,0:T(8,128)(2,1)}, u32[]{:S(2)}) copy-start(bf16[1024,3328]{1,0:T(8,128)(2,1)} %param.12) | copy-start | bytes 20447236
  9.7 5.0 %collective-permute-start = (bf16[1664,512]{1,0:T(8,128)(2,1)S(1)}, bf16[1664,512]{1,0:T(8,128)(2,1)S(1)}, u32[]{:S(2)}, u32[]{:S(2)}) collective-permute-start(bf16[1664,512]{1,0:T(8,128)(2,1)S(1)} %other_core.2), channel_id=1, source_target_pairs={{0,8},{8,0},{1,9},{9,1},{2,10},{10,2},{3,11},{11,3},{4,12},{12,4},... | collective-permute-start | bytes 5111816 | tf_op jit(solution)/shard_map/ppermute | solution.py:35
  14.1 3.9 %collective-permute-start.5 = (bf16[1664,512]{1,0:T(8,128)(2,1)S(1)}, bf16[1664,512]{1,0:T(8,128)(2,1)S(1)}, u32[]{:S(2)}, u32[]{:S(2)}) collective-permute-start(bf16[1664,512]{1,0:T(8,128)(2,1)S(1)} %other_core.3), channel_id=1, source_target_pairs={{0,8},{8,0},{1,9},{9,1},{2,10},{10,2},{3,11},{11,3},{4,12},{12,4},... | collective-permute-start | bytes 5111816 | tf_op jit(solution)/shard_map/ppermute | solution.py:35
  14.7 27.3 %slice-start = ((s8[6815744]{0:T(1024)(128)(4,1)}), s8[2621440]{0:T(1024)(128)(4,1)S(1)}, s32[]{:S(2)}) async-start(s8[6815744]{0:T(1024)(128)(4,1)} %bitcast.18), calls=%async_computation.2 | async-start | bytes 5242880
  15.1 22.5 %collective-permute-start.1 = (bf16[832,512]{1,0:T(8,128)(2,1)S(1)}, bf16[832,512]{1,0:T(8,128)(2,1)S(1)}, u32[]{:S(2)}, u32[]{:S(2)}) collective-permute-start(bf16[832,512]{1,0:T(8,128)(2,1)S(1)} %get-tuple-element.27), channel_id=1, source_target_pairs={{0,64},{64,0},{1,65},{65,1},{2,66},{66,2},{3,67},{67,3},{4,68},{68... | collective-permute-start | bytes 2555912 | tf_op jit(solution)/shard_map/ppermute | solution.py:35
  18.1 24.0 %slice-start.1 = ((s8[6815744]{0:T(1024)(128)(4,1)}), s8[4194304]{0:T(1024)(128)(4,1)S(1)}, s32[]{:S(2)}) async-start(s8[6815744]{0:T(1024)(128)(4,1)} %bitcast.18), calls=%async_computation.3 | async-start | bytes 8388608
  18.9 18.8 %collective-permute-start.6 = (bf16[832,512]{1,0:T(8,128)(2,1)S(1)}, bf16[832,512]{1,0:T(8,128)(2,1)S(1)}, u32[]{:S(2)}, u32[]{:S(2)}) collective-permute-start(bf16[832,512]{1,0:T(8,128)(2,1)S(1)} %get-tuple-element.34), channel_id=1, source_target_pairs={{0,16},{8,56},{16,0},{24,40},{32,48},{40,24},{48,32},{56,8},{1,17}... | collective-permute-start | bytes 2555912 | tf_op jit(solution)/shard_map/ppermute | solution.py:49
  20.8 3.8 %collective-permute-start.7 = (bf16[2,48,128]{2,1,0:T(8,128)(2,1)S(1)}, bf16[2,48,128]{2,1,0:T(8,128)(2,1)S(1)}, u32[]{:S(2)}, u32[]{:S(2)}) collective-permute-start(bf16[2,48,128]{2,1,0:T(8,128)(2,1)S(1)} %double.3.refs_1_.refs_3_.refs_0_), channel_id=1, source_target_pairs={{0,2},{2,0},{4,6},{6,4},{1,3},{3,1},{5,7},{7,5},{8,10},{10,8},{12,... | collective-permute-start | bytes 73736 | tf_op jit(solution)/shard_map/ppermute | solution.py:53
  24.7 5.6 %collective-permute-start.8 = (bf16[4,48,128]{2,1,0:T(8,128)(2,1)S(1)}, bf16[4,48,128]{2,1,0:T(8,128)(2,1)S(1)}, u32[]{:S(2)}, u32[]{:S(2)}) collective-permute-start(bf16[4,48,128]{2,1,0:T(8,128)(2,1)S(1)} %double.4.refs_0_), channel_id=1, source_target_pairs={{0,6},{2,4},{4,2},{6,0},{1,7},{3,5},{5,3},{7,1},{8,14},{10,12},{12... | collective-permute-start | bytes 147464 | tf_op jit(solution)/shard_map/ppermute | solution.py:53
  30.7 1.3 %collective-permute-start.9 = (f32[32,512]{1,0:T(8,128)S(1)}, f32[32,512]{1,0:T(8,128)S(1)}, u32[]{:S(2)}, u32[]{:S(2)}) collective-permute-start(f32[32,512]{1,0:T(8,128)S(1)} %fusion.refs_0_), channel_id=1, source_target_pairs={{0,8},{8,0},{1,9},{9,1},{2,10},{10,2},{3,11},{11,3},{4,12},{12,4},... | collective-permute-start | bytes 196616 | tf_op jit(solution)/shard_map/ppermute | solution.py:35
  32.0 5.7 %collective-permute-start.10 = (f32[32,512]{1,0:T(8,128)S(1)}, f32[32,512]{1,0:T(8,128)S(1)}, u32[]{:S(2)}, u32[]{:S(2)}) collective-permute-start(f32[32,512]{1,0:T(8,128)S(1)} %add.1.refs_2_), channel_id=1, source_target_pairs={{0,16},{8,56},{16,0},{24,40},{32,48},{40,24},{48,32},{56,8},{1,17}... | collective-permute-start | bytes 196616 | tf_op jit(solution)/shard_map/ppermute | solution.py:49
  37.9 14.2 %collective-permute-start.11 = (bf16[448,512]{1,0:T(8,128)(2,1)S(1)}, bf16[448,512]{1,0:T(8,128)(2,1)S(1)}, u32[]{:S(2)}, u32[]{:S(2)}) collective-permute-start(bf16[448,512]{1,0:T(8,128)(2,1)S(1)} %get-tuple-element.37), channel_id=1, source_target_pairs={{0,48},{8,24},{16,32},{24,8},{32,16},{40,56},{48,0},{56,40},{1,49}... | collective-permute-start | bytes 1376264 | tf_op jit(solution)/shard_map/ppermute | solution.py:49
  42.0 20.4 %copy-start.1 = (bf16[208,16]{0,1:T(8,128)(2,1)S(1)}, bf16[208,16]{0,1:T(8,128)(2,1)}, u32[]{:S(2)}) copy-start(bf16[208,16]{0,1:T(8,128)(2,1)} %param.16) | copy-start | bytes 19972
  42.0 20.4 %copy-start.2 = (bf16[208,16]{0,1:T(8,128)(2,1)S(1)}, bf16[208,16]{0,1:T(8,128)(2,1)}, u32[]{:S(2)}) copy-start(bf16[208,16]{0,1:T(8,128)(2,1)} %param.17) | copy-start | bytes 19972
  42.0 20.4 %copy-start.3 = (bf16[16,208]{1,0:T(8,128)(2,1)S(1)}, bf16[16,208]{1,0:T(8,128)(2,1)}, u32[]{:S(2)}) copy-start(bf16[16,208]{1,0:T(8,128)(2,1)} %refs_6_.1) | copy-start | bytes 19972
  42.0 13.1 %collective-permute-start.2 = (bf16[416,512]{1,0:T(8,128)(2,1)S(1)}, bf16[416,512]{1,0:T(8,128)(2,1)S(1)}, u32[]{:S(2)}, u32[]{:S(2)}) collective-permute-start(bf16[416,512]{1,0:T(8,128)(2,1)S(1)} %get-tuple-element.29), channel_id=1, source_target_pairs={{0,16},{8,56},{16,0},{24,40},{32,48},{40,24},{48,32},{56,8},{1,17}... | collective-permute-start | bytes 1277960 | tf_op jit(solution)/shard_map/ppermute | solution.py:49
  52.2 10.2 %collective-permute-start.12 = (bf16[240,512]{1,0:T(8,128)(2,1)S(1)}, bf16[240,512]{1,0:T(8,128)(2,1)S(1)}, u32[]{:S(2)}, u32[]{:S(2)}) collective-permute-start(bf16[240,512]{1,0:T(8,128)(2,1)S(1)} %get-tuple-element.40), channel_id=1, source_target_pairs={{0,64},{64,0},{1,65},{65,1},{2,66},{66,2},{3,67},{67,3},{4,68},{68... | collective-permute-start | bytes 737288 | tf_op jit(solution)/shard_map/ppermute | solution.py:35
  55.3 7.1 %collective-permute-start.3 = (bf16[208,512]{1,0:T(8,128)(2,1)S(1)}, bf16[208,512]{1,0:T(8,128)(2,1)S(1)}, u32[]{:S(2)}, u32[]{:S(2)}) collective-permute-start(bf16[208,512]{1,0:T(8,128)(2,1)S(1)} %get-tuple-element.31), channel_id=1, source_target_pairs={{0,48},{8,24},{16,32},{24,8},{32,16},{40,56},{48,0},{56,40},{1,49}... | collective-permute-start | bytes 638984 | tf_op jit(solution)/shard_map/ppermute | solution.py:49
  88.5 3.8 %collective-permute-start.13 = (bf16[8,224,512]{2,1,0:T(8,128)(2,1)S(1)}, bf16[8,224,512]{2,1,0:T(8,128)(2,1)S(1)}, u32[]{:S(2)}, u32[]{:S(2)}) collective-permute-start(bf16[8,224,512]{2,1,0:T(8,128)(2,1)S(1)} %all_to_all.10.refs_0_), channel_id=1, source_target_pairs={{0,8},{8,0},{1,9},{9,1},{2,10},{10,2},{3,11},{11,3},{4,12},{12,4},... | collective-permute-start | bytes 5505032 | tf_op jit(solution)/shard_map/ppermute | solution.py:35

commit v2 on v1

--- a/solution.py
+++ b/solution.py
@@ -14,7 +14,7 @@
 FSDP = ("yh", "z", "c")
 TP = ("x", "yl")
 RANK = 16
-VMEM_LIMIT = 16 * 1024 * 1024
+VMEM_LIMIT = 12 * 1024 * 1024
 
 
 def pair_bits(core):

time: 116 us -> 116 us (level)
  no operation moved by 1% of the time
where the time goes in v2:
time: 116 us
  blocking collectives  45.3 us (39%)
  waiting for transfers between devices  23.5 us (20%)
  starting transfers between devices  21.9 us (19%)
  matrix products  15.8 us (14%)
  Pallas kernels  8.02 us (7%)
    all_to_all x2, blocking collectives, exchange(): return lax.all_to_all(value, axes, split_axis=0, concat_axis=0)  45.3 us
    dot_general x2, matrix products, per_device(): lax.dot_general(w, states, (((0,), (1,)), ((), ())), preferred_element_ty...  11.2 us
    ppermute x5, waiting for transfers between devices, ring_pair(): return lax.ppermute(value, axes, moves)  10.7 us
    ppermute x5, starting transfers between devices, ring_pair(): return lax.ppermute(value, axes, moves)  9.02 us
    ppermute x7, starting transfers between devices, swap(): return lax.ppermute(value, axis, [(0, 1), (1, 0)])  8.64 us
    ppermute x7, waiting for transfers between devices, swap(): return lax.ppermute(value, axis, [(0, 1), (1, 0)])  7.65 us
    ppermute x2, waiting for transfers between devices, xor_pair(): return lax.ppermute(value, axis, [(i, i ^ step) for i in range(4)])  5.15 us
    ppermute x2, starting transfers between devices, xor_pair(): return lax.ppermute(value, axis, [(i, i ^ step) for i in range(4)])  4.26 us
  transfers between devices with their start and end apart: 14, of which 7 were waited for; matrix products, arithmetic and copies ran while one was open for 12% of the time, Pallas kernels for 5%

profile of v2, /device:TPU:0, one launch (start us, length us, event | category | flops | bytes accessed | tf_op | source)
XLA Modules:
  0.0 115.5 jit_solution(9902318182040717280)
XLA Ops:
  0.0 0.0 copy-start
  0.0 0.8 maximum_bitcast_fusion.refs_0_
  0.8 1.7 %collective-permute-start.4 = (bf16[1,48,128]{2,1,0:T(8,128)(2,1)S(1)}, bf16[1,48,128]{2,1,0:T(8,128)(2,1)S(1)}, u32[]{:S(2)}, u32[]{:S(2)}) collective-permute-start(bf16[1,48,128]{2,1,0:T(8,128)(2,1)S(1)} %maximum_bitcast_fusion.refs_0_), channel_id=1, source_target_pairs={{0,1},{1,0},{2,3},{3,2},{4,5},{5,4},{6,7},{7,6},{8,9},{9,8},{10,11... | collective-permute-start | bytes 36872 | tf_op jit(solution)/shard_map/ppermute | solution.py:35
  2.5 0.0 copy-done
  2.5 0.0 copy-start.4
  2.5 7.1 %convolution_convert_fusion.1.refs_0_ = bf16[3328,512]{1,0:T(8,128)(2,1)S(1)} fusion(bf16[1024,3328]{1,0:T(8,128)(2,1)} %param.11, bf16[512,1024]{1,0:T(8,128)(2,1)S(1)} %bitcast.15), kind=kOutput, calls=%fused_computation.1 | convolution fusion | flops 3491364864 | bytes 11272192 | tf_op jit(solution)/shard_map/dot_general | solution.py:269
  9.6 0.1 other_core.2
  9.7 0.1 collective-permute-start
  9.8 0.0 copy-done.4
  9.8 4.1 %convolution_convert_fusion.refs_0_ = bf16[3328,512]{1,0:T(8,128)(2,1)S(1)} fusion(bf16[1024,3328]{1,0:T(8,128)(2,1)S(1)} %copy-done.4, bf16[512,1024]{1,0:T(8,128)(2,1)S(1)} %bitcast.16), kind=kOutput, calls=%fused_computation | convolution fusion | flops 3491364864 | bytes 11272192 | tf_op jit(solution)/shard_map/dot_general | solution.py:269
  14.0 0.0 collective-permute-done.4.refs_1_
  14.0 0.1 other_core.3
  14.1 0.6 collective-permute-start.5
  14.7 0.0 collective-permute-done.refs_1_
  14.7 0.0 slice-start
  14.7 0.4 core_sum.2
  15.1 3.0 %collective-permute-start.1 = (bf16[832,512]{1,0:T(8,128)(2,1)S(1)}, bf16[832,512]{1,0:T(8,128)(2,1)S(1)}, u32[]{:S(2)}, u32[]{:S(2)}) collective-permute-start(bf16[832,512]{1,0:T(8,128)(2,1)S(1)} %get-tuple-element.27), channel_id=1, source_target_pairs={{0,64},{64,0},{1,65},{65,1},{2,66},{66,2},{3,67},{67,3},{4,68},{68... | collective-permute-start | bytes 2555912 | tf_op jit(solution)/shard_map/ppermute | solution.py:35
  18.0 0.0 collective-permute-done.5.refs_1_
  18.1 0.0 slice-start.1
  18.1 0.9 core_sum.3
  18.9 1.9 %collective-permute-start.6 = (bf16[832,512]{1,0:T(8,128)(2,1)S(1)}, bf16[832,512]{1,0:T(8,128)(2,1)S(1)}, u32[]{:S(2)}, u32[]{:S(2)}) collective-permute-start(bf16[832,512]{1,0:T(8,128)(2,1)S(1)} %get-tuple-element.34), channel_id=1, source_target_pairs={{0,16},{8,56},{16,0},{24,40},{32,48},{40,24},{48,32},{56,8},{1,17}... | collective-permute-start | bytes 2555912 | tf_op jit(solution)/shard_map/ppermute | solution.py:49
  20.8 1.5 %collective-permute-start.7 = (bf16[2,48,128]{2,1,0:T(8,128)(2,1)S(1)}, bf16[2,48,128]{2,1,0:T(8,128)(2,1)S(1)}, u32[]{:S(2)}, u32[]{:S(2)}) collective-permute-start(bf16[2,48,128]{2,1,0:T(8,128)(2,1)S(1)} %double.3.refs_1_.refs_3_.refs_0_), channel_id=1, source_target_pairs={{0,2},{2,0},{4,6},{6,4},{1,3},{3,1},{5,7},{7,5},{8,10},{10,8},{12,... | collective-permute-start | bytes 73736 | tf_op jit(solution)/shard_map/ppermute | solution.py:53
  22.3 2.3 %collective-permute-done.7.refs_1_ = bf16[2,48,128]{2,1,0:T(8,128)(2,1)S(1)} collective-permute-done((bf16[2,48,128]{2,1,0:T(8,128)(2,1)S(1)}, bf16[2,48,128]{2,1,0:T(8,128)(2,1)S(1)}, u32[]{:S(2)}, u32[]{:S(2)}) %collective-permute-start.7) | collective-permute-done | bytes 24608 | tf_op jit(solution)/shard_map/ppermute | solution.py:53
  24.7 2.8 %collective-permute-start.8 = (bf16[4,48,128]{2,1,0:T(8,128)(2,1)S(1)}, bf16[4,48,128]{2,1,0:T(8,128)(2,1)S(1)}, u32[]{:S(2)}, u32[]{:S(2)}) collective-permute-start(bf16[4,48,128]{2,1,0:T(8,128)(2,1)S(1)} %double.4.refs_0_), channel_id=1, source_target_pairs={{0,6},{2,4},{4,2},{6,0},{1,7},{3,5},{5,3},{7,1},{8,14},{10,12},{12... | collective-permute-start | bytes 147464 | tf_op jit(solution)/shard_map/ppermute | solution.py:53
  27.4 2.8 %collective-permute-done.8.refs_1_ = bf16[4,48,128]{2,1,0:T(8,128)(2,1)S(1)} collective-permute-done((bf16[4,48,128]{2,1,0:T(8,128)(2,1)S(1)}, bf16[4,48,128]{2,1,0:T(8,128)(2,1)S(1)}, u32[]{:S(2)}, u32[]{:S(2)}) %collective-permute-start.8) | collective-permute-done | bytes 49184 | tf_op jit(solution)/shard_map/ppermute | solution.py:53
  30.3 0.4 fusion.refs_0_
  30.7 0.4 collective-permute-start.9
  31.1 0.9 collective-permute-done.9.refs_1_
  32.0 0.4 collective-permute-start.10
  32.4 5.2 %collective-permute-done.1.refs_1_ = bf16[832,512]{1,0:T(8,128)(2,1)S(1)} collective-permute-done((bf16[832,512]{1,0:T(8,128)(2,1)S(1)}, bf16[832,512]{1,0:T(8,128)(2,1)S(1)}, u32[]{:S(2)}, u32[]{:S(2)}) %collective-permute-start.1) | collective-permute-done | bytes 852000 | tf_op jit(solution)/shard_map/ppermute | solution.py:35
  37.5 0.2 halve.4
  37.7 0.0 collective-permute-done.10.refs_3_
  37.7 0.0 collective-permute-done.6.refs_1_
  37.8 0.1 halve.6
  37.9 4.1 %collective-permute-start.11 = (bf16[448,512]{1,0:T(8,128)(2,1)S(1)}, bf16[448,512]{1,0:T(8,128)(2,1)S(1)}, u32[]{:S(2)}, u32[]{:S(2)}) collective-permute-start(bf16[448,512]{1,0:T(8,128)(2,1)S(1)} %get-tuple-element.37), channel_id=1, source_target_pairs={{0,48},{8,24},{16,32},{24,8},{32,16},{40,56},{48,0},{56,40},{1,49}... | collective-permute-start | bytes 1376264 | tf_op jit(solution)/shard_map/ppermute | solution.py:49
  42.0 0.0 copy-start.1
  42.0 0.0 copy-start.2
  42.0 0.0 copy-start.3
  42.0 0.0 collective-permute-start.2
  42.0 0.0 slice-done
  42.0 0.0 slice-done.1
  42.1 3.9 %down_rows.1 = (bf16[1664,1024]{1,0:T(8,128)(2,1)S(1)}, bf16[1664,1024]{1,0:T(8,128)(2,1)S(1)}, f32[8,128]{1,0:T(8,128)S(1)}) custom-call(bf16[3328,1024]{1,0:T(8,128)(2,1)S(1)} %bitcast.19), custom_call_target="tpu_custom_call" | custom-call | bytes 13631488 | tf_op jit(solution)/shard_map/down_rows/pallas_call | solution.py:204
  45.9 6.2 %collective-permute-done.11.refs_1_ = bf16[448,512]{1,0:T(8,128)(2,1)S(1)} collective-permute-done((bf16[448,512]{1,0:T(8,128)(2,1)S(1)}, bf16[448,512]{1,0:T(8,128)(2,1)S(1)}, u32[]{:S(2)}, u32[]{:S(2)}) %collective-permute-start.11) | collective-permute-done | bytes 458784 | tf_op jit(solution)/shard_map/ppermute | solution.py:49
  52.1 0.1 halve.7
  52.2 3.0 %collective-permute-start.12 = (bf16[240,512]{1,0:T(8,128)(2,1)S(1)}, bf16[240,512]{1,0:T(8,128)(2,1)S(1)}, u32[]{:S(2)}, u32[]{:S(2)}) collective-permute-start(bf16[240,512]{1,0:T(8,128)(2,1)S(1)} %get-tuple-element.40), channel_id=1, source_target_pairs={{0,64},{64,0},{1,65},{65,1},{2,66},{66,2},{3,67},{67,3},{4,68},{68... | collective-permute-start | bytes 737288 | tf_op jit(solution)/shard_map/ppermute | solution.py:35
  55.2 0.0 collective-permute-done.2.refs_1_
  55.2 0.1 halve.5
  55.3 2.6 %collective-permute-start.3 = (bf16[208,512]{1,0:T(8,128)(2,1)S(1)}, bf16[208,512]{1,0:T(8,128)(2,1)S(1)}, u32[]{:S(2)}, u32[]{:S(2)}) collective-permute-start(bf16[208,512]{1,0:T(8,128)(2,1)S(1)} %get-tuple-element.31), channel_id=1, source_target_pairs={{0,48},{8,24},{16,32},{24,8},{32,16},{40,56},{48,0},{56,40},{1,49}... | collective-permute-start | bytes 638984 | tf_op jit(solution)/shard_map/ppermute | solution.py:49
  57.9 4.5 %collective-permute-done.3.refs_1_ = bf16[208,512]{1,0:T(8,128)(2,1)S(1)} collective-permute-done((bf16[208,512]{1,0:T(8,128)(2,1)S(1)}, bf16[208,512]{1,0:T(8,128)(2,1)S(1)}, u32[]{:S(2)}, u32[]{:S(2)}) %collective-permute-start.3) | collective-permute-done | bytes 213024 | tf_op jit(solution)/shard_map/ppermute | solution.py:49
  62.4 0.0 collective-permute-done.12.refs_3_
  62.4 0.0 copy-done.1
  62.4 0.0 copy-done.2
  62.4 0.0 copy-done.3
  62.4 0.6 hidden.1
  63.0 25.5 %all_to_all.10.refs_0_ = bf16[8,224,512]{2,1,0:T(8,128)(2,1)S(1)} all-to-all(bf16[8,224,512]{2,1,0:T(8,128)(2,1)S(1)} %hidden.1), channel_id=1, replica_groups=mesh['yh'=2,'z'=4,'c'=2,'x'=4,'yl'=2] {'yh','z'}, dimensions={0} | all-to-all | bytes 3670016 | tf_op jit(solution)/shard_map/all_to_all | solution.py:57
  88.5 0.0 collective-permute-start.13
  88.5 0.1 strip.2
  88.7 2.1 %fusion.2.refs_0_ = f32[512,1024]{1,0:T(8,128)S(1)} fusion(bf16[1664,512]{1,0:T(8,128)(2,1)S(1)} %get-tuple-element.41, bf16[1664,1024]{1,0:T(8,128)(2,1)S(1)} %get-tuple-element.42), kind=kOutput, calls=%fused_computation.5 | convolution fusion | flops 1744830464 | bytes 7208960 | tf_op jit(solution)/shard_map/dot_general | solution.py:335
  90.7 1.6 %collective-permute-done.13.refs_0_ = bf16[8,224,512]{2,1,0:T(8,128)(2,1)S(1)} collective-permute-done((bf16[8,224,512]{2,1,0:T(8,128)(2,1)S(1)}, bf16[8,224,512]{2,1,0:T(8,128)(2,1)S(1)}, u32[]{:S(2)}, u32[]{:S(2)}) %collective-permute-start.13) | collective-permute-done | bytes 1835040 | tf_op jit(solution)/shard_map/ppermute | solution.py:35
  92.3 0.1 strip.3
  92.4 2.1 %fusion.3.refs_2_ = f32[512,1024]{1,0:T(8,128)S(1)} fusion(bf16[1664,512]{1,0:T(8,128)(2,1)S(1)} %get-tuple-element.44, bf16[1664,1024]{1,0:T(8,128)(2,1)S(1)} %get-tuple-element.45), kind=kOutput, calls=%fused_computation.6 | convolution fusion | flops 1744830464 | bytes 7208960 | tf_op jit(solution)/shard_map/dot_general | solution.py:335
  94.5 0.5 tp_blocks.1
  95.0 19.7 %all_to_all.11.refs_0_ = bf16[8,2,32,1024]{3,2,1,0:T(8,128)(2,1)S(1)} all-to-all(bf16[8,2,32,1024]{3,2,1,0:T(8,128)(2,1)S(1)} %tp_blocks.1), channel_id=1, replica_groups=mesh['yh'=2,'z'=4,'c'=2,'x'=4,'yl'=2] {'x','yl'}, dimensions={0} | all-to-all | bytes 2097152 | tf_op jit(solution)/shard_map/all_to_all | solution.py:57
  114.7 0.8 owner_sum.1
  (5 shorter events, 0.1 us)
Async XLA Ops:
  0.0 2.5 %copy-start = (bf16[2,256,1024]{2,1,0:T(8,128)(2,1)S(1)}, bf16[2,256,1024]{2,1,0:T(8,128)(2,1)}, u32[]{:S(2)}) copy-start(bf16[2,256,1024]{2,1,0:T(8,128)(2,1)} %param.10) | copy-start | bytes 3145732
  0.8 13.2 %collective-permute-start.4 = (bf16[1,48,128]{2,1,0:T(8,128)(2,1)S(1)}, bf16[1,48,128]{2,1,0:T(8,128)(2,1)S(1)}, u32[]{:S(2)}, u32[]{:S(2)}) collective-permute-start(bf16[1,48,128]{2,1,0:T(8,128)(2,1)S(1)} %maximum_bitcast_fusion.refs_0_), channel_id=1, source_target_pairs={{0,1},{1,0},{2,3},{3,2},{4,5},{5,4},{6,7},{7,6},{8,9},{9,8},{10,11... | collective-permute-start | bytes 36872 | tf_op jit(solution)/shard_map/ppermute | solution.py:35
  2.5 7.3 %copy-start.4 = (bf16[1024,3328]{1,0:T(8,128)(2,1)S(1)}, bf16[1024,3328]{1,0:T(8,128)(2,1)}, u32[]{:S(2)}) copy-start(bf16[1024,3328]{1,0:T(8,128)(2,1)} %param.12) | copy-start | bytes 20447236
  9.7 5.0 %collective-permute-start = (bf16[1664,512]{1,0:T(8,128)(2,1)S(1)}, bf16[1664,512]{1,0:T(8,128)(2,1)S(1)}, u32[]{:S(2)}, u32[]{:S(2)}) collective-permute-start(bf16[1664,512]{1,0:T(8,128)(2,1)S(1)} %other_core.2), channel_id=1, source_target_pairs={{0,8},{8,0},{1,9},{9,1},{2,10},{10,2},{3,11},{11,3},{4,12},{12,4},... | collective-permute-start | bytes 5111816 | tf_op jit(solution)/shard_map/ppermute | solution.py:35
  14.1 3.9 %collective-permute-start.5 = (bf16[1664,512]{1,0:T(8,128)(2,1)S(1)}, bf16[1664,512]{1,0:T(8,128)(2,1)S(1)}, u32[]{:S(2)}, u32[]{:S(2)}) collective-permute-start(bf16[1664,512]{1,0:T(8,128)(2,1)S(1)} %other_core.3), channel_id=1, source_target_pairs={{0,8},{8,0},{1,9},{9,1},{2,10},{10,2},{3,11},{11,3},{4,12},{12,4},... | collective-permute-start | bytes 5111816 | tf_op jit(solution)/shard_map/ppermute | solution.py:35
  14.7 27.3 %slice-start = ((s8[6815744]{0:T(1024)(128)(4,1)}), s8[2621440]{0:T(1024)(128)(4,1)S(1)}, s32[]{:S(2)}) async-start(s8[6815744]{0:T(1024)(128)(4,1)} %bitcast.18), calls=%async_computation.2 | async-start | bytes 5242880
  15.1 22.5 %collective-permute-start.1 = (bf16[832,512]{1,0:T(8,128)(2,1)S(1)}, bf16[832,512]{1,0:T(8,128)(2,1)S(1)}, u32[]{:S(2)}, u32[]{:S(2)}) collective-permute-start(bf16[832,512]{1,0:T(8,128)(2,1)S(1)} %get-tuple-element.27), channel_id=1, source_target_pairs={{0,64},{64,0},{1,65},{65,1},{2,66},{66,2},{3,67},{67,3},{4,68},{68... | collective-permute-start | bytes 2555912 | tf_op jit(solution)/shard_map/ppermute | solution.py:35
  18.1 24.0 %slice-start.1 = ((s8[6815744]{0:T(1024)(128)(4,1)}), s8[4194304]{0:T(1024)(128)(4,1)S(1)}, s32[]{:S(2)}) async-start(s8[6815744]{0:T(1024)(128)(4,1)} %bitcast.18), calls=%async_computation.3 | async-start | bytes 8388608
  18.9 18.8 %collective-permute-start.6 = (bf16[832,512]{1,0:T(8,128)(2,1)S(1)}, bf16[832,512]{1,0:T(8,128)(2,1)S(1)}, u32[]{:S(2)}, u32[]{:S(2)}) collective-permute-start(bf16[832,512]{1,0:T(8,128)(2,1)S(1)} %get-tuple-element.34), channel_id=1, source_target_pairs={{0,16},{8,56},{16,0},{24,40},{32,48},{40,24},{48,32},{56,8},{1,17}... | collective-permute-start | bytes 2555912 | tf_op jit(solution)/shard_map/ppermute | solution.py:49
  20.8 3.8 %collective-permute-start.7 = (bf16[2,48,128]{2,1,0:T(8,128)(2,1)S(1)}, bf16[2,48,128]{2,1,0:T(8,128)(2,1)S(1)}, u32[]{:S(2)}, u32[]{:S(2)}) collective-permute-start(bf16[2,48,128]{2,1,0:T(8,128)(2,1)S(1)} %double.3.refs_1_.refs_3_.refs_0_), channel_id=1, source_target_pairs={{0,2},{2,0},{4,6},{6,4},{1,3},{3,1},{5,7},{7,5},{8,10},{10,8},{12,... | collective-permute-start | bytes 73736 | tf_op jit(solution)/shard_map/ppermute | solution.py:53
  24.7 5.6 %collective-permute-start.8 = (bf16[4,48,128]{2,1,0:T(8,128)(2,1)S(1)}, bf16[4,48,128]{2,1,0:T(8,128)(2,1)S(1)}, u32[]{:S(2)}, u32[]{:S(2)}) collective-permute-start(bf16[4,48,128]{2,1,0:T(8,128)(2,1)S(1)} %double.4.refs_0_), channel_id=1, source_target_pairs={{0,6},{2,4},{4,2},{6,0},{1,7},{3,5},{5,3},{7,1},{8,14},{10,12},{12... | collective-permute-start | bytes 147464 | tf_op jit(solution)/shard_map/ppermute | solution.py:53
  30.7 1.3 %collective-permute-start.9 = (f32[32,512]{1,0:T(8,128)S(1)}, f32[32,512]{1,0:T(8,128)S(1)}, u32[]{:S(2)}, u32[]{:S(2)}) collective-permute-start(f32[32,512]{1,0:T(8,128)S(1)} %fusion.refs_0_), channel_id=1, source_target_pairs={{0,8},{8,0},{1,9},{9,1},{2,10},{10,2},{3,11},{11,3},{4,12},{12,4},... | collective-permute-start | bytes 196616 | tf_op jit(solution)/shard_map/ppermute | solution.py:35
  32.0 5.7 %collective-permute-start.10 = (f32[32,512]{1,0:T(8,128)S(1)}, f32[32,512]{1,0:T(8,128)S(1)}, u32[]{:S(2)}, u32[]{:S(2)}) collective-permute-start(f32[32,512]{1,0:T(8,128)S(1)} %add.1.refs_2_), channel_id=1, source_target_pairs={{0,16},{8,56},{16,0},{24,40},{32,48},{40,24},{48,32},{56,8},{1,17}... | collective-permute-start | bytes 196616 | tf_op jit(solution)/shard_map/ppermute | solution.py:49
  37.9 14.2 %collective-permute-start.11 = (bf16[448,512]{1,0:T(8,128)(2,1)S(1)}, bf16[448,512]{1,0:T(8,128)(2,1)S(1)}, u32[]{:S(2)}, u32[]{:S(2)}) collective-permute-start(bf16[448,512]{1,0:T(8,128)(2,1)S(1)} %get-tuple-element.37), channel_id=1, source_target_pairs={{0,48},{8,24},{16,32},{24,8},{32,16},{40,56},{48,0},{56,40},{1,49}... | collective-permute-start | bytes 1376264 | tf_op jit(solution)/shard_map/ppermute | solution.py:49
  42.0 20.4 %copy-start.1 = (bf16[208,16]{0,1:T(8,128)(2,1)S(1)}, bf16[208,16]{0,1:T(8,128)(2,1)}, u32[]{:S(2)}) copy-start(bf16[208,16]{0,1:T(8,128)(2,1)} %param.16) | copy-start | bytes 19972
  42.0 20.4 %copy-start.2 = (bf16[208,16]{0,1:T(8,128)(2,1)S(1)}, bf16[208,16]{0,1:T(8,128)(2,1)}, u32[]{:S(2)}) copy-start(bf16[208,16]{0,1:T(8,128)(2,1)} %param.17) | copy-start | bytes 19972
  42.0 20.4 %copy-start.3 = (bf16[16,208]{1,0:T(8,128)(2,1)S(1)}, bf16[16,208]{1,0:T(8,128)(2,1)}, u32[]{:S(2)}) copy-start(bf16[16,208]{1,0:T(8,128)(2,1)} %refs_6_.1) | copy-start | bytes 19972
  42.0 13.1 %collective-permute-start.2 = (bf16[416,512]{1,0:T(8,128)(2,1)S(1)}, bf16[416,512]{1,0:T(8,128)(2,1)S(1)}, u32[]{:S(2)}, u32[]{:S(2)}) collective-permute-start(bf16[416,512]{1,0:T(8,128)(2,1)S(1)} %get-tuple-element.29), channel_id=1, source_target_pairs={{0,16},{8,56},{16,0},{24,40},{32,48},{40,24},{48,32},{56,8},{1,17}... | collective-permute-start | bytes 1277960 | tf_op jit(solution)/shard_map/ppermute | solution.py:49
  52.2 10.2 %collective-permute-start.12 = (bf16[240,512]{1,0:T(8,128)(2,1)S(1)}, bf16[240,512]{1,0:T(8,128)(2,1)S(1)}, u32[]{:S(2)}, u32[]{:S(2)}) collective-permute-start(bf16[240,512]{1,0:T(8,128)(2,1)S(1)} %get-tuple-element.40), channel_id=1, source_target_pairs={{0,64},{64,0},{1,65},{65,1},{2,66},{66,2},{3,67},{67,3},{4,68},{68... | collective-permute-start | bytes 737288 | tf_op jit(solution)/shard_map/ppermute | solution.py:35
  55.3 7.1 %collective-permute-start.3 = (bf16[208,512]{1,0:T(8,128)(2,1)S(1)}, bf16[208,512]{1,0:T(8,128)(2,1)S(1)}, u32[]{:S(2)}, u32[]{:S(2)}) collective-permute-start(bf16[208,512]{1,0:T(8,128)(2,1)S(1)} %get-tuple-element.31), channel_id=1, source_target_pairs={{0,48},{8,24},{16,32},{24,8},{32,16},{40,56},{48,0},{56,40},{1,49}... | collective-permute-start | bytes 638984 | tf_op jit(solution)/shard_map/ppermute | solution.py:49
  88.5 3.8 %collective-permute-start.13 = (bf16[8,224,512]{2,1,0:T(8,128)(2,1)S(1)}, bf16[8,224,512]{2,1,0:T(8,128)(2,1)S(1)}, u32[]{:S(2)}, u32[]{:S(2)}) collective-permute-start(bf16[8,224,512]{2,1,0:T(8,128)(2,1)S(1)} %all_to_all.10.refs_0_), channel_id=1, source_target_pairs={{0,8},{8,0},{1,9},{9,1},{2,10},{10,2},{3,11},{11,3},{4,12},{12,4},... | collective-permute-start | bytes 5505032 | tf_op jit(solution)/shard_map/ppermute | solution.py:35
